TPU v7x, 32 devices: a whole 2x2x4 slice. The times are simulated.
32 devices in a mesh: tile: 8 (over z, y), lev: 4 (over x, core).
Axes of the slice: x: 2, y: 2, z: 4, core: 2. Of those that a mesh axis runs over, the one named last changes fastest.
Arguments:
- cotangent: bfloat16 [3072, 128, 128], P('lev', 'tile'), may hold values from -6 to 6
- mix_weight: bfloat16 [3072, 3072], P(None, 'tile'), may hold values from -0.109375 to 0.109375
- kernel: float32 [3072, 9], P('lev'), may hold values from -2 to 2
- send_rows: int32 [8, 8, 41], P('tile'), may hold values from -1 to 291, as said below
- recv_cells: int32 [8, 8, 41], P('tile'), may hold values from -1 to 1918, as said below
- recv_weight: float32 [8, 4, 8, 41], P('tile'), may hold values from 0 to 1, as said below
Outputs:
- grad_input: bfloat16 [3072, 128, 128], P('lev', 'tile')
Inputs may be any that keep to these rules, and one draw needn't show every extreme that they name: `send_rows`: partner d is always a strip of the other panel. Every slot of the side columns (with the four corners) of strip s appears exactly once over all d and k, the slots of row 0 only for the strip at place 0 of a panel and those of row 17 only for the strip at place 4 - 1; no other slots appear. Used entries of a block come first, and some pair uses all 41. recv_cells[d, s, k] is -1 exactly where send_rows[s, d, k] is -1; otherwise its row is at most 14 and its column at most 126, so all four corners lie in strip d; the largest cell is reached. `recv_weight`: the four weights of an entry are the bilinear weights of a point in the donor cell and sum to one.
All inputs are finite; a program needn't handle non-finite values.
Results may differ from a plain program's by a relative error of at most 0.0049.
Values may be sent and summed in bfloat16 or wider, within the bound.
A program may use at most 128 MiB of HBM per device.

v0:
```python
import jax
import jax.numpy as jnp
from jax import lax
from jax.sharding import PartitionSpec as P


def padded_2(cells, sides, width):
    for axis, dim in sides:
        count = lax.axis_size(axis)
        head = lax.slice_in_dim(cells, 0, width, axis=dim)
        tail = lax.slice_in_dim(cells, cells.shape[dim] - width, cells.shape[dim], axis=dim)
        cells = jnp.concatenate(
            [
                lax.ppermute(tail, axis, [(i, (i + 1) % count) for i in range(count)]),
                cells,
                lax.ppermute(head, axis, [((i + 1) % count, i) for i in range(count)]),
            ],
            axis=dim,
        )
    return cells


def stencil_adjoint(grad_block, kernel):
    feat_local, tile_rows, tile_cols = grad_block.shape
    padded = jnp.pad(grad_block.astype(jnp.float32), ((0, 0), (2, 2), (2, 2)))
    summed = jnp.zeros((feat_local, tile_rows + 2, tile_cols + 2), jnp.float32)
    for row_shift in (-1, 0, 1):
        for col_shift in (-1, 0, 1):
            kernel_tap = kernel[:, 3 * (row_shift + 1) + col_shift + 1]
            window_part = padded[
                :,
                1 - row_shift : 3 - row_shift + tile_rows,
                1 - col_shift : 3 - col_shift + tile_cols,
            ]
            summed = summed + kernel_tap[:, None, None] * window_part
    return summed


def cycle_of(extended):
    return jnp.concatenate(
        [extended[:, 0, :], extended[:, -1, :], extended[:, 1:-1, 0], extended[:, 1:-1, -1]], axis=1
    )


def deposit(running, values, cell_index, weight_rows, row_length):
    is_used = cell_index >= 0
    base_cell = jnp.maximum(cell_index, 0)
    spread = values.astype(jnp.float32)
    for corner, offset in enumerate((0, 1, row_length, row_length + 1)):
        running = running.at[:, base_cell + offset].add(
            spread * jnp.where(is_used, weight_rows[corner], 0.0)[None, :]
        )
    return running


def per_device(cotangent, mix_weight, kernel, send_rows, recv_cells, recv_weight):
    feat_local, tile_rows, tile_cols = cotangent.shape
    cell_count = tile_rows * tile_cols
    flat_grad = cotangent.reshape(feat_local, cell_count)
    level_index = lax.axis_index("lev")
    own_rows = lax.dynamic_slice_in_dim(mix_weight, level_index * feat_local, feat_local, 0)
    weight_rows = lax.all_gather(own_rows, "tile", axis=1, tiled=True)
    grad_mix = jnp.dot(
        weight_rows,
        lax.all_gather(flat_grad, "lev", axis=0, tiled=True),
        preferred_element_type=jnp.float32,
    ).astype(jnp.bfloat16)
    extended = stencil_adjoint(grad_mix.reshape(feat_local, tile_rows, tile_cols), kernel)
    cycle_values = cycle_of(extended).astype(jnp.bfloat16)
    tile_count = lax.axis_size("tile")
    strip_count = tile_count // 2
    tile_here = lax.axis_index("tile")
    place_index = (tile_here + strip_count // 2) % tile_count % strip_count
    keep_top = (place_index != 0).astype(jnp.float32)
    keep_bottom = (place_index != strip_count - 1).astype(jnp.float32)
    edge_rows = jnp.stack(
        [extended[:, 0, 1:-1] * keep_top, extended[:, -1, 1:-1] * keep_bottom], axis=1
    )
    bordered = padded_2(edge_rows.astype(jnp.bfloat16), (("tile", 1),), 1).astype(edge_rows.dtype)
    interior = extended[:, 1:-1, 1:-1]
    interior = interior.at[:, 0, :].add(bordered[:, 0, :]).at[:, -1, :].add(bordered[:, 3, :])
    running = interior.reshape(feat_local, cell_count)
    cell_lists = recv_cells[0]
    weight_lists = recv_weight[0]
    slot_lists = lax.all_to_all(send_rows[0], "tile", split_axis=0, concat_axis=0, tiled=True)
    cycle_size = cycle_values.shape[1]
    shard_piece = lax.all_gather(cycle_values, "tile", axis=1, tiled=True)
    sources = shard_piece.shape[1] // cycle_size
    local_slots = (
        jnp.arange(sources, dtype=jnp.int32)[:, None] * cycle_size + jnp.maximum(slot_lists, 0)
    ).reshape(-1)
    values = jnp.take(shard_piece, local_slots, axis=1)
    cells_part = cell_lists.reshape(-1)
    weights_part = weight_lists.reshape(4, -1)
    running = deposit(running, values, cells_part, weights_part, tile_cols)
    return running.reshape(feat_local, tile_rows, tile_cols).astype(jnp.bfloat16)


def solution(mesh):
    in_specs = (
        P("lev", "tile", None),
        P(None, "tile"),
        P("lev", None),
        P("tile", None, None),
        P("tile", None, None),
        P("tile", None, None, None),
    )
    out_specs = P("lev", "tile", None)
    return jax.shard_map(
        per_device, mesh=mesh, in_specs=in_specs, out_specs=out_specs, check_vma=False
    )
```

profile of v0, /device:TPU:0, one launch (start us, length us, event | category | flops | bytes accessed | tf_op | source)
XLA Modules:
  0.0 363.0 jit_solution(4709097112009996498)
XLA Ops:
  6.5 1.7 copy-done
  9.1 4.9 %copy.22 = bf16[96,8,16,128]{3,1,2,0:T(8,128)(2,1)} copy(bf16[96,8,16,128]{3,2,1,0:T(8,128)(2,1)} %bitcast.36) | data formatting | bytes 6291456
  14.2 79.0 %all-gather.5.cloned.1.call-done = bf16[768,3072]{1,0:T(8,128)(2,1)} async-done(((bf16[768,384]{1,0:T(8,128)(2,1)}), bf16[768,3072]{1,0:T(8,128)(2,1)}) %all-gather.5.cloned.1.call-update) | async-done | bytes 4718608 | tf_op jit(solution)/shard_map/all_gather | solution.py:62
  93.2 81.9 %all-gather.7.cloned.1.call-done = bf16[3072,2048]{1,0:T(8,128)(2,1)} async-done(((bf16[768,2048]{1,0:T(8,128)(2,1)}), bf16[3072,2048]{1,0:T(8,128)(2,1)}) %all-gather.7.cloned.1.call-update) | async-done | bytes 12582928 | tf_op jit(solution)/shard_map/all_gather | solution.py:65
  175.0 15.4 %convolution_convert_fusion = bf16[768,2048]{1,0:T(8,128)(2,1)} fusion(bf16[768,3072]{1,0:T(8,128)(2,1)} %all-gather.5.cloned.1.call-done, bf16[3072,2048]{1,0:T(8,128)(2,1)} %all-gather.7.cloned.1.call-done), kind=kOutput, calls=%fused_computation.23 | convolution fusion | flops 9665249280 | bytes 20447232 | tf_op jit(solution)/shard_map/dot_general | solution.py:63
  190.4 4.7 %copy.15 = bf16[768,2048]{0,1:T(8,128)(2,1)} copy(bf16[768,2048]{1,0:T(8,128)(2,1)} %convolution_convert_fusion) | data formatting | bytes 6291456 | tf_op jit(solution)/shard_map/convert_element_type | solution.py:25
  195.1 5.8 %pad_convert_fusion = f32[768,20,132]{0,2,1:T(8,128)} fusion(bf16[768,16,128]{0,2,1:T(8,128)(2,1)} %bitcast.34), kind=kLoop, calls=%fused_computation.22 | loop fusion | flops 2027520 | bytes 11255808 | tf_op jit(solution)/shard_map/jit(_pad)/pad | solution.py:25
  200.9 28.3 %fusion.25 = (bf16[768,18,130]{0,2,1:T(8,128)(2,1)}, f32[768,18,130]{0,2,1:T(8,128)}) fusion(f32[768,20,132]{0,2,1:T(8,128)} %pad_convert_fusion, f32[768]{0:T(1024)S(1)} %get-tuple-element.36, f32[768]{0:T(1024)S(1)} %get-tuple-element.37, f32[768]{0:T(1024)S(1)} %get-tuple-element.30, f32[768]{0:T(1024)S(1)} %get-tuple-element.31, ...), kind=kLoop, calls=%fused_computation.90 | loop fusion | flops 32348160 | bytes 75506688 | tf_op jit(solution)/shard_map/convert.14
  232.3 5.5 %all-to-all-start = ((s32[8,1,41]{2,1,0:T(1,128)}), s32[8,1,41]{2,1,0:T(1,128)S(1)}, u32[]{:S(2)}, u32[]{:S(2)}) async-start(s32[8,1,41]{2,1,0:T(1,128)} %bitcast.2), calls=%async_computation | async-start | bytes 8192 | tf_op jit(solution)/shard_map/all_to_all | solution.py:85
  239.2 5.0 %all-to-all-done = s32[8,1,41]{2,1,0:T(1,128)S(1)} async-done(((s32[8,1,41]{2,1,0:T(1,128)}), s32[8,1,41]{2,1,0:T(1,128)S(1)}, u32[]{:S(2)}, u32[]{:S(2)}) %all-to-all-start) | async-done | bytes 1344 | tf_op jit(solution)/shard_map/all_to_all | solution.py:85
  246.2 4.2 %collective-permute-start.1 = (bf16[768,1,128]{0,2,1:T(8,128)(2,1)S(1)}, bf16[768,1,128]{0,2,1:T(8,128)(2,1)S(1)}, u32[]{:S(2)}, u32[]{:S(2)}) collective-permute-start(bf16[768,1,128]{0,2,1:T(8,128)(2,1)S(1)} %get-tuple-element.41), channel_id=1, source_target_pairs={{4,0},{8,4},{12,8},{16,12},{20,16},{24,20},{28,24},{0,28},{5,1},{9... | collective-permute-start | bytes 589832 | tf_op jit(solution)/shard_map/ppermute | solution.py:16
  250.4 6.3 %slice.198 = f32[768,16,128]{0,2,1:T(8,128)} slice(f32[768,18,130]{0,2,1:T(8,128)} %get-tuple-element.39), slice={[0:768], [1:17], [1:129]} | slice | bytes 12582912 | tf_op jit(solution)/shard_map/slice | solution.py:80
  256.7 2.9 collective-permute-done
  259.6 1.8 fusion.17
  261.4 1.8 fusion.16
  263.2 40.2 %all-gather.9.cloned.1.call-done = bf16[8,292,768]{2,1,0:T(8,128)(2,1)} async-done(((bf16[1,292,768]{2,1,0:T(8,128)(2,1)}), bf16[8,292,768]{2,1,0:T(8,128)(2,1)}) %all-gather.9.cloned.1.call-update) | async-done | bytes 3588112 | tf_op jit(solution)/shard_map/all_gather | solution.py:87
  303.4 4.7 %reshape.290 = bf16[2336,768]{1,0:T(8,128)(2,1)} reshape(bf16[8,292,768]{2,1,0:T(8,128)(2,1)} %all-gather.9.cloned.1.call-done) | data formatting | bytes 7176192
  308.1 5.0 %gather_fusion = bf16[328,768]{1,0:T(8,128)(2,1)S(1)} fusion(bf16[768,2336]{0,1:T(8,128)(2,1)} %bitcast.32, s32[1024]{0:T(1024)S(1)} %pad_clamp_fusion), kind=kCustom, calls=%fused_computation | custom fusion | bytes 1008928 | tf_op jit(solution)/shard_map/jit(_take)/gather | solution.py:92
  313.1 8.4 %scatter_custom_fusion = f32[768,2048]{0,1:T(8,128)} fusion(f32[768,2048]{0,1:T(8,128)} %bitcast.1, s32[328]{0:T(512)S(1)} %reshape.246, f32[328]{0:T(512)S(1)} %get-tuple-element.62, bf16[328,768]{1,0:T(8,128)(2,1)S(1)} %gather_fusion, pred[328]{0:T(512)(128)(4,1)S(1)} %compare_and_fusion), kind=kCustom, calls=%fused_computation.30 | custom fusion | flops 1007616 | bytes 6797824 | tf_op jit(solution)/shard_map/scatter-add | solution.py:50
  321.4 8.4 %scatter_custom_fusion.1 = f32[768,2048]{0,1:T(8,128)} fusion(f32[768,2048]{0,1:T(8,128)} %scatter_custom_fusion, s32[328]{0:T(512)S(1)} %fusion.21, f32[328]{0:T(512)S(1)} %get-tuple-element.61, bf16[328,768]{1,0:T(8,128)(2,1)S(1)} %gather_fusion, pred[328]{0:T(512)(128)(4,1)S(1)} %compare_and_fusion), kind=kCustom, calls=%fused_computation.31 | custom fusion | flops 1007616 | bytes 6797824 | tf_op jit(solution)/shard_map/scatter-add | solution.py:50
  329.8 8.4 %scatter_custom_fusion.2 = f32[768,2048]{0,1:T(8,128)} fusion(f32[768,2048]{0,1:T(8,128)} %scatter_custom_fusion.1, s32[328]{0:T(512)S(1)} %fusion.22, f32[328]{0:T(512)S(1)} %get-tuple-element.60, bf16[328,768]{1,0:T(8,128)(2,1)S(1)} %gather_fusion, pred[328]{0:T(512)(128)(4,1)S(1)} %compare_and_fusion), kind=kCustom, calls=%fused_computation.32 | custom fusion | flops 1007616 | bytes 6797824 | tf_op jit(solution)/shard_map/scatter-add | solution.py:50
  338.2 8.5 %scatter_custom_fusion.3 = f32[768,2048]{0,1:T(8,128)} fusion(f32[768,2048]{0,1:T(8,128)} %scatter_custom_fusion.2, s32[328]{0:T(512)S(1)} %fusion.23, f32[328]{0:T(512)S(1)} %get-tuple-element.59, bf16[328,768]{1,0:T(8,128)(2,1)S(1)} %gather_fusion, pred[328]{0:T(512)(128)(4,1)S(1)} %compare_and_fusion), kind=kCustom, calls=%fused_computation.29 | custom fusion | flops 1007616 | bytes 6797824 | tf_op jit(solution)/shard_map/scatter-add | solution.py:50
  346.7 4.8 %convert_element_type.35 = bf16[768,2048]{0,1:T(8,128)(2,1)} convert(f32[768,2048]{0,1:T(8,128)} %scatter_custom_fusion.3) | non-fusion elementwise | flops 1572864 | bytes 9437184 | tf_op jit(solution)/shard_map/convert_element_type | solution.py:96
  351.5 5.0 %copy.14 = bf16[768,16,128]{2,1,0:T(8,128)(2,1)} copy(bf16[768,16,128]{0,2,1:T(8,128)(2,1)} %bitcast.35) | data formatting | bytes 6291456 | tf_op jit(solution)/shard_map/convert_element_type | solution.py:96
  (53 shorter events, 7.4 us)
Async XLA Ops:
  6.5 1.7 copy-start
  6.5 7.5 %copy-start.4 = (f32[768,9]{0,1:T(8,128)S(1)}, f32[768,9]{0,1:T(8,128)}, u32[]{:S(2)}) copy-start(f32[768,9]{0,1:T(8,128)} %param.12) | copy-start | bytes 82948
  6.5 86.6 %all-gather.5.cloned.1.call-start = ((), (), s32[]{:S(2)}) async-start(), calls=%async_computation.1 | async-start | bytes 5308416 | tf_op jit(solution)/shard_map/all_gather | solution.py:62
  9.1 165.9 %all-gather.7.cloned.1.call-start = ((), (), s32[]{:S(2)}) async-start(), calls=%async_computation.2 | async-start | bytes 15728640 | tf_op jit(solution)/shard_map/all_gather | solution.py:65
  14.0 289.4 %all-gather.9.cloned.1.call-start = ((), (), s32[]{:S(2)}) async-start(), calls=%async_computation.3 | async-start | bytes 4091904 | tf_op jit(solution)/shard_map/all_gather | solution.py:87
  200.9 36.8 %copy-start.2 = (f32[1,4,8,41]{3,2,1,0:T(8,128)S(1)}, f32[1,4,8,41]{3,2,1,0:T(8,128)}, u32[]{:S(2)}) copy-start(f32[1,4,8,41]{3,2,1,0:T(8,128)} %param.15) | copy-start | bytes 15748
  200.9 37.2 %copy-start.3 = (s32[1,8,41]{2,1,0:T(8,128)S(1)}, s32[1,8,41]{2,1,0:T(8,128)}, u32[]{:S(2)}) copy-start(s32[1,8,41]{2,1,0:T(8,128)} %param.14) | copy-start | bytes 3940
  232.3 11.9 %all-to-all-start = ((s32[8,1,41]{2,1,0:T(1,128)}), s32[8,1,41]{2,1,0:T(1,128)S(1)}, u32[]{:S(2)}, u32[]{:S(2)}) async-start(s32[8,1,41]{2,1,0:T(1,128)} %bitcast.2), calls=%async_computation | async-start | bytes 8192 | tf_op jit(solution)/shard_map/all_to_all | solution.py:85
  245.6 14.0 %collective-permute-start = (bf16[768,1,128]{0,2,1:T(8,128)(2,1)S(1)}, bf16[768,1,128]{0,2,1:T(8,128)(2,1)S(1)}, u32[]{:S(2)}, u32[]{:S(2)}) collective-permute-start(bf16[768,1,128]{0,2,1:T(8,128)(2,1)S(1)} %get-tuple-element.40), channel_id=1, source_target_pairs={{0,4},{4,8},{8,12},{12,16},{16,20},{20,24},{24,28},{28,0},{1,5},{5... | collective-permute-start | bytes 589832 | tf_op jit(solution)/shard_map/ppermute | solution.py:14
  246.2 13.4 %collective-permute-start.1 = (bf16[768,1,128]{0,2,1:T(8,128)(2,1)S(1)}, bf16[768,1,128]{0,2,1:T(8,128)(2,1)S(1)}, u32[]{:S(2)}, u32[]{:S(2)}) collective-permute-start(bf16[768,1,128]{0,2,1:T(8,128)(2,1)S(1)} %get-tuple-element.41), channel_id=1, source_target_pairs={{4,0},{8,4},{12,8},{16,12},{20,16},{24,20},{28,24},{0,28},{5,1},{9... | collective-permute-start | bytes 589832 | tf_op jit(solution)/shard_map/ppermute | solution.py:16
  338.2 18.3 %copy-start.1 = (bf16[3072,384]{1,0:T(8,128)(2,1)S(1)}, bf16[3072,384]{1,0:T(8,128)(2,1)}, u32[]{:S(2)}) copy-start(bf16[3072,384]{1,0:T(8,128)(2,1)} %param.11) | copy-start | bytes 7077892
Sparse Core Ops, SparseCore 0:
  9.4 83.6 all-gather.4
  94.7 80.2 all-gather.6
  232.4 70.9 all-gather.8
where the time goes:
time: 364 us; the launch traced here: 363 us
  waiting for transfers between devices  209 us (57%)
  other arithmetic  78.3 us (22%)
  local copies, waits for them, and re-layouts  36.6 us (10%)
  matrix products  15.4 us (4%)
  between operations  13.3 us (4%)
  starting transfers between devices  10.4 us (3%)
    all_gather x1, waiting for transfers between devices, per_device(): lax.all_gather(flat_grad, 'lev', axis=0, tiled=True)  81.9 us
    all_gather x1, waiting for transfers between devices, per_device(): weight_rows = lax.all_gather(own_rows, 'tile', axis=1, tiled=True)  79 us
    all_gather x1, waiting for transfers between devices, per_device(): shard_piece = lax.all_gather(cycle_values, 'tile', axis=1, tiled=True)  40.2 us
    scatter-add x4, other arithmetic, deposit(): running.at[:, base_cell + offset]  33.6 us
    another operation x1, other arithmetic  28.3 us
    dot_general x1, matrix products, per_device(): jnp.dot(weight_rows, lax.all_gather(flat_grad, 'lev', axis=0, tiled=True)...  15.4 us
    unnamed x13, local copies, waits for them, and re-layouts  11.3 us
  transfers between devices with their start and end apart: 6, of which 5 were waited for; matrix products, arithmetic and copies ran while one was open for 5% of the time, Pallas kernels for 0%

commit v1 on v0

--- a/solution.py
+++ b/solution.py
@@ -59,7 +59,12 @@
     flat_grad = cotangent.reshape(feat_local, cell_count)
     level_index = lax.axis_index("lev")
     own_rows = lax.dynamic_slice_in_dim(mix_weight, level_index * feat_local, feat_local, 0)
-    weight_rows = lax.all_gather(own_rows, "tile", axis=1, tiled=True)
+    ring = [own_rows]
+    for hop in range(7):
+        ring.append(lax.ppermute(ring[-1], "tile", [(dev, (dev + 1) % 8) for dev in range(8)]))
+    weight_rows = jnp.roll(
+        jnp.concatenate(ring[::-1], axis=1), (lax.axis_index("tile") + 1) * ring[0].shape[1], axis=1
+    )
     grad_mix = jnp.dot(
         weight_rows,
         lax.all_gather(flat_grad, "lev", axis=0, tiled=True),

time: 364 us -> 317 us (0.87)
  waiting for transfers between devices: 209 us -> 150 us
  local copies, waits for them, and re-layouts: 36.6 us -> 51.2 us
  other arithmetic: 78.3 us -> 74.5 us
    ppermute x0 -> x7, waiting for transfers between devices: none -> 104 us  [per_device(): lax.ppermute(ring[-1], 'tile', [(dev, (dev + 1) % 8) for dev in range(8)])]
    all_gather x1, waiting for transfers between devices: 81.9 us -> 0.01 us  [per_device(): lax.all_gather(flat_grad, 'lev', axis=0, tiled=True)]
    all_gather x1 -> x0, waiting for transfers between devices: 79 us -> none  [per_device(): weight_rows = lax.all_gather(own_rows, 'tile', axis=1, tiled=True)]
    unnamed x13 -> x34, local copies, waits for them, and re-layouts: 11.3 us -> 26.1 us
  transfers between devices with their start and end apart: 6 -> 12, of which waited for: 5 -> 10; matrix products, arithmetic and copies ran while one was open for 5% -> 10% of each run, Pallas kernels for 0% -> 0%
where the time goes in v1:
time: 317 us; the launch traced here: 316 us
  waiting for transfers between devices  150 us (47%)
  other arithmetic  74.5 us (24%)
  local copies, waits for them, and re-layouts  51.2 us (16%)
  matrix products  15.5 us (5%)
  between operations  13.6 us (4%)
  starting transfers between devices  11.2 us (4%)
    ppermute x7, waiting for transfers between devices, per_device(): lax.ppermute(ring[-1], 'tile', [(dev, (dev + 1) % 8) for dev in range(8)])  104 us
    all_gather x1, waiting for transfers between devices, per_device(): shard_piece = lax.all_gather(cycle_values, 'tile', axis=1, tiled=True)  38.8 us
    scatter-add x4, other arithmetic, deposit(): running.at[:, base_cell + offset]  33.5 us
    another operation x1, other arithmetic  28.2 us
    unnamed x34, local copies, waits for them, and re-layouts  26.1 us
    dot_general x1, matrix products, per_device(): jnp.dot(weight_rows, lax.all_gather(flat_grad, 'lev', axis=0, tiled=True)...  15.5 us
  transfers between devices with their start and end apart: 12, of which 10 were waited for; matrix products, arithmetic and copies ran while one was open for 10% of the time, Pallas kernels for 0%

profile of v1, /device:TPU:0, one launch (start us, length us, event | category | flops | bytes accessed | tf_op | source)
XLA Modules:
  0.0 315.8 jit_solution(10847949527223112144)
XLA Ops:
  6.5 4.9 %copy.22 = bf16[96,8,16,128]{3,1,2,0:T(8,128)(2,1)} copy(bf16[96,8,16,128]{3,2,1,0:T(8,128)(2,1)} %bitcast.35) | data formatting | bytes 6291456
  15.6 16.4 %collective-permute-done = bf16[768,384]{1,0:T(8,128)(2,1)S(1)} collective-permute-done((bf16[768,384]{1,0:T(8,128)(2,1)S(1)}, bf16[768,384]{1,0:T(8,128)(2,1)S(1)}, u32[]{:S(2)}, u32[]{:S(2)}) %collective-permute-start) | collective-permute-done | bytes 589856 | tf_op jit(solution)/shard_map/ppermute | solution.py:64
  32.0 17.2 %collective-permute-done.1 = bf16[768,384]{1,0:T(8,128)(2,1)S(1)} collective-permute-done((bf16[768,384]{1,0:T(8,128)(2,1)S(1)}, bf16[768,384]{1,0:T(8,128)(2,1)S(1)}, u32[]{:S(2)}, u32[]{:S(2)}) %collective-permute-start.1) | collective-permute-done | bytes 589856 | tf_op jit(solution)/shard_map/ppermute | solution.py:64
  49.2 16.3 %collective-permute-done.2 = bf16[768,384]{1,0:T(8,128)(2,1)S(1)} collective-permute-done((bf16[768,384]{1,0:T(8,128)(2,1)S(1)}, bf16[768,384]{1,0:T(8,128)(2,1)S(1)}, u32[]{:S(2)}, u32[]{:S(2)}) %collective-permute-start.2) | collective-permute-done | bytes 589856 | tf_op jit(solution)/shard_map/ppermute | solution.py:64
  65.5 15.4 %collective-permute-done.3 = bf16[768,384]{1,0:T(8,128)(2,1)S(1)} collective-permute-done((bf16[768,384]{1,0:T(8,128)(2,1)S(1)}, bf16[768,384]{1,0:T(8,128)(2,1)S(1)}, u32[]{:S(2)}, u32[]{:S(2)}) %collective-permute-start.3) | collective-permute-done | bytes 589856 | tf_op jit(solution)/shard_map/ppermute | solution.py:64
  80.9 14.4 %collective-permute-done.4 = bf16[768,384]{1,0:T(8,128)(2,1)S(1)} collective-permute-done((bf16[768,384]{1,0:T(8,128)(2,1)S(1)}, bf16[768,384]{1,0:T(8,128)(2,1)S(1)}, u32[]{:S(2)}, u32[]{:S(2)}) %collective-permute-start.4) | collective-permute-done | bytes 589856 | tf_op jit(solution)/shard_map/ppermute | solution.py:64
  95.3 13.5 %collective-permute-done.5 = bf16[768,384]{1,0:T(8,128)(2,1)S(1)} collective-permute-done((bf16[768,384]{1,0:T(8,128)(2,1)S(1)}, bf16[768,384]{1,0:T(8,128)(2,1)S(1)}, u32[]{:S(2)}, u32[]{:S(2)}) %collective-permute-start.5) | collective-permute-done | bytes 589856 | tf_op jit(solution)/shard_map/ppermute | solution.py:64
  110.6 11.0 %collective-permute-done.6 = bf16[768,384]{1,0:T(8,128)(2,1)} collective-permute-done((bf16[768,384]{1,0:T(8,128)(2,1)S(1)}, bf16[768,384]{1,0:T(8,128)(2,1)}, u32[]{:S(2)}, u32[]{:S(2)}) %collective-permute-start.6) | collective-permute-done | bytes 589856 | tf_op jit(solution)/shard_map/ppermute | solution.py:64
  138.9 15.5 %fusion.10 = bf16[768,2048]{1,0:T(8,128)(2,1)} fusion(bf16[3072,2048]{1,0:T(8,128)(2,1)} %all-gather.4.cloned.1.call-done, bf16[768,6144]{1,0:T(8,128)(2,1)} %constant_dynamic-update-slice_fusion, s32[]{:T(128)S(6)} %select_n.108), kind=kOutput, calls=%fused_computation.25 | convolution fusion | flops 9665249280 | bytes 20447236 | tf_op jit(solution)/shard_map/dot_general | solution.py:68
  154.5 3.2 %copy.15 = bf16[768,2048]{0,1:T(8,128)(2,1)S(1)} copy(bf16[768,2048]{1,0:T(8,128)(2,1)} %fusion.10) | data formatting | bytes 6291456 | tf_op jit(solution)/shard_map/convert_element_type | solution.py:25
  157.7 4.0 %pad_convert_fusion = f32[768,20,132]{0,2,1:T(8,128)} fusion(bf16[768,16,128]{0,2,1:T(8,128)(2,1)S(1)} %bitcast.33), kind=kLoop, calls=%fused_computation.24 | loop fusion | flops 2027520 | bytes 11255808 | tf_op jit(solution)/shard_map/jit(_pad)/pad | solution.py:25
  161.7 28.2 %fusion.31 = (bf16[768,18,130]{0,2,1:T(8,128)(2,1)}, f32[768,18,130]{0,2,1:T(8,128)}) fusion(f32[768,20,132]{0,2,1:T(8,128)} %pad_convert_fusion, f32[768]{0:T(1024)S(1)} %copy-done.4, f32[768]{0:T(1024)S(1)} %copy-done.5, f32[768]{0:T(1024)S(1)} %get-tuple-element.30, f32[768]{0:T(1024)S(1)} %get-tuple-element.31, f32[768]{0:T(1024)S(1)} %get-tuple-element.32, ...), kind=kLoop, calls=%fused_computation.109 | loop fusion | flops 32348160 | bytes 75506688 | tf_op jit(solution)/shard_map/convert.14
  193.0 3.3 %all-to-all-start = ((s32[8,1,41]{2,1,0:T(1,128)}), s32[8,1,41]{2,1,0:T(1,128)S(1)}, u32[]{:S(2)}, u32[]{:S(2)}) async-start(s32[8,1,41]{2,1,0:T(1,128)} %bitcast.2), calls=%async_computation | async-start | bytes 8192 | tf_op jit(solution)/shard_map/all_to_all | solution.py:90
  197.7 5.1 %all-to-all-done = s32[8,1,41]{2,1,0:T(1,128)S(1)} async-done(((s32[8,1,41]{2,1,0:T(1,128)}), s32[8,1,41]{2,1,0:T(1,128)S(1)}, u32[]{:S(2)}, u32[]{:S(2)}) %all-to-all-start) | async-done | bytes 1344 | tf_op jit(solution)/shard_map/all_to_all | solution.py:90
  204.8 4.2 %collective-permute-start.8 = (bf16[768,1,128]{0,2,1:T(8,128)(2,1)S(1)}, bf16[768,1,128]{0,2,1:T(8,128)(2,1)S(1)}, u32[]{:S(2)}, u32[]{:S(2)}) collective-permute-start(bf16[768,1,128]{0,2,1:T(8,128)(2,1)S(1)} %get-tuple-element.41), channel_id=1, source_target_pairs={{4,0},{8,4},{12,8},{16,12},{20,16},{24,20},{28,24},{0,28},{5,1},{9... | collective-permute-start | bytes 589832 | tf_op jit(solution)/shard_map/ppermute | solution.py:16
  209.1 6.3 %slice.198 = f32[768,16,128]{0,2,1:T(8,128)} slice(f32[768,18,130]{0,2,1:T(8,128)} %get-tuple-element.39), slice={[0:768], [1:17], [1:129]} | slice | bytes 12582912 | tf_op jit(solution)/shard_map/slice | solution.py:85
  220.5 38.8 %all-gather.6.cloned.1.call-done = bf16[8,292,768]{2,1,0:T(8,128)(2,1)} async-done(((bf16[1,292,768]{2,1,0:T(8,128)(2,1)}), bf16[8,292,768]{2,1,0:T(8,128)(2,1)}) %all-gather.6.cloned.1.call-update) | async-done | bytes 3588112 | tf_op jit(solution)/shard_map/all_gather | solution.py:92
  259.3 4.7 %reshape.290 = bf16[2336,768]{1,0:T(8,128)(2,1)} reshape(bf16[8,292,768]{2,1,0:T(8,128)(2,1)} %all-gather.6.cloned.1.call-done) | data formatting | bytes 7176192
  264.0 5.0 %gather_fusion = bf16[328,768]{1,0:T(8,128)(2,1)S(1)} fusion(bf16[768,2336]{0,1:T(8,128)(2,1)} %bitcast.31, s32[1024]{0:T(1024)S(1)} %pad_clamp_fusion), kind=kCustom, calls=%fused_computation | custom fusion | bytes 1008928 | tf_op jit(solution)/shard_map/jit(_take)/gather | solution.py:97
  269.0 8.4 %scatter_custom_fusion = f32[768,2048]{0,1:T(8,128)} fusion(f32[768,2048]{0,1:T(8,128)} %bitcast.1, s32[328]{0:T(512)S(1)} %reshape.246, f32[328]{0:T(512)S(1)} %get-tuple-element.62, bf16[328,768]{1,0:T(8,128)(2,1)S(1)} %gather_fusion, pred[328]{0:T(512)(128)(4,1)S(1)} %compare_and_fusion), kind=kCustom, calls=%fused_computation.32 | custom fusion | flops 1007616 | bytes 6797824 | tf_op jit(solution)/shard_map/scatter-add | solution.py:50
  277.4 8.4 %scatter_custom_fusion.1 = f32[768,2048]{0,1:T(8,128)} fusion(f32[768,2048]{0,1:T(8,128)} %scatter_custom_fusion, s32[328]{0:T(512)S(1)} %get-tuple-element.64, f32[328]{0:T(512)S(1)} %get-tuple-element.61, bf16[328,768]{1,0:T(8,128)(2,1)S(1)} %gather_fusion, pred[328]{0:T(512)(128)(4,1)S(1)} %compare_and_fusion), kind=kCustom, calls=%fused_computation.33 | custom fusion | flops 1007616 | bytes 6797824 | tf_op jit(solution)/shard_map/scatter-add | solution.py:50
  285.7 8.4 %scatter_custom_fusion.2 = f32[768,2048]{0,1:T(8,128)} fusion(f32[768,2048]{0,1:T(8,128)} %scatter_custom_fusion.1, s32[328]{0:T(512)S(1)} %fusion.27, f32[328]{0:T(512)S(1)} %get-tuple-element.60, bf16[328,768]{1,0:T(8,128)(2,1)S(1)} %gather_fusion, pred[328]{0:T(512)(128)(4,1)S(1)} %compare_and_fusion), kind=kCustom, calls=%fused_computation.34 | custom fusion | flops 1007616 | bytes 6797824 | tf_op jit(solution)/shard_map/scatter-add | solution.py:50
  294.1 8.4 %scatter_custom_fusion.3 = f32[768,2048]{0,1:T(8,128)} fusion(f32[768,2048]{0,1:T(8,128)} %scatter_custom_fusion.2, s32[328]{0:T(512)S(1)} %fusion.28, f32[328]{0:T(512)S(1)} %get-tuple-element.59, bf16[328,768]{1,0:T(8,128)(2,1)S(1)} %gather_fusion, pred[328]{0:T(512)(128)(4,1)S(1)} %compare_and_fusion), kind=kCustom, calls=%fused_computation.31 | custom fusion | flops 1007616 | bytes 6797824 | tf_op jit(solution)/shard_map/scatter-add | solution.py:50
  305.6 3.4 %copy.14 = bf16[768,16,128]{2,1,0:T(8,128)(2,1)} copy(bf16[768,16,128]{0,2,1:T(8,128)(2,1)S(1)} %bitcast.34) | data formatting | bytes 6291456 | tf_op jit(solution)/shard_map/convert_element_type | solution.py:101
  (85 shorter events, 37.8 us)
Async XLA Ops:
  6.5 132.4 %all-gather.4.cloned.1.call-start = ((), (), s32[]{:S(2)}) async-start(), calls=%async_computation.1 | async-start | bytes 15728640 | tf_op jit(solution)/shard_map/all_gather | solution.py:70
  11.4 247.9 %all-gather.6.cloned.1.call-start = ((), (), s32[]{:S(2)}) async-start(), calls=%async_computation.2 | async-start | bytes 4091904 | tf_op jit(solution)/shard_map/all_gather | solution.py:92
  12.6 19.4 %collective-permute-start = (bf16[768,384]{1,0:T(8,128)(2,1)S(1)}, bf16[768,384]{1,0:T(8,128)(2,1)S(1)}, u32[]{:S(2)}, u32[]{:S(2)}) collective-permute-start(bf16[768,384]{1,0:T(8,128)(2,1)S(1)} %constant_dynamic-slice_fusion), channel_id=1, source_target_pairs={{0,4},{4,8},{8,12},{12,16},{16,20},{20,24},{24,28},{28,0},{1,5},{5... | collective-permute-start | bytes 1769480 | tf_op jit(solution)/shard_map/ppermute | solution.py:64
  32.0 17.2 %collective-permute-start.1 = (bf16[768,384]{1,0:T(8,128)(2,1)S(1)}, bf16[768,384]{1,0:T(8,128)(2,1)S(1)}, u32[]{:S(2)}, u32[]{:S(2)}) collective-permute-start(bf16[768,384]{1,0:T(8,128)(2,1)S(1)} %collective-permute-done), channel_id=1, source_target_pairs={{0,4},{4,8},{8,12},{12,16},{16,20},{20,24},{24,28},{28,0},{1,5},{5... | collective-permute-start | bytes 1769480 | tf_op jit(solution)/shard_map/ppermute | solution.py:64
  49.2 16.3 %collective-permute-start.2 = (bf16[768,384]{1,0:T(8,128)(2,1)S(1)}, bf16[768,384]{1,0:T(8,128)(2,1)S(1)}, u32[]{:S(2)}, u32[]{:S(2)}) collective-permute-start(bf16[768,384]{1,0:T(8,128)(2,1)S(1)} %collective-permute-done.1), channel_id=1, source_target_pairs={{0,4},{4,8},{8,12},{12,16},{16,20},{20,24},{24,28},{28,0},{1,5},{5... | collective-permute-start | bytes 1769480 | tf_op jit(solution)/shard_map/ppermute | solution.py:64
  65.5 15.4 %collective-permute-start.3 = (bf16[768,384]{1,0:T(8,128)(2,1)S(1)}, bf16[768,384]{1,0:T(8,128)(2,1)S(1)}, u32[]{:S(2)}, u32[]{:S(2)}) collective-permute-start(bf16[768,384]{1,0:T(8,128)(2,1)S(1)} %collective-permute-done.2), channel_id=1, source_target_pairs={{0,4},{4,8},{8,12},{12,16},{16,20},{20,24},{24,28},{28,0},{1,5},{5... | collective-permute-start | bytes 1769480 | tf_op jit(solution)/shard_map/ppermute | solution.py:64
  80.9 14.4 %collective-permute-start.4 = (bf16[768,384]{1,0:T(8,128)(2,1)S(1)}, bf16[768,384]{1,0:T(8,128)(2,1)S(1)}, u32[]{:S(2)}, u32[]{:S(2)}) collective-permute-start(bf16[768,384]{1,0:T(8,128)(2,1)S(1)} %collective-permute-done.3), channel_id=1, source_target_pairs={{0,4},{4,8},{8,12},{12,16},{16,20},{20,24},{24,28},{28,0},{1,5},{5... | collective-permute-start | bytes 1769480 | tf_op jit(solution)/shard_map/ppermute | solution.py:64
  95.3 13.5 %collective-permute-start.5 = (bf16[768,384]{1,0:T(8,128)(2,1)S(1)}, bf16[768,384]{1,0:T(8,128)(2,1)S(1)}, u32[]{:S(2)}, u32[]{:S(2)}) collective-permute-start(bf16[768,384]{1,0:T(8,128)(2,1)S(1)} %collective-permute-done.4), channel_id=1, source_target_pairs={{0,4},{4,8},{8,12},{12,16},{16,20},{20,24},{24,28},{28,0},{1,5},{5... | collective-permute-start | bytes 1769480 | tf_op jit(solution)/shard_map/ppermute | solution.py:64
  108.8 12.7 %collective-permute-start.6 = (bf16[768,384]{1,0:T(8,128)(2,1)S(1)}, bf16[768,384]{1,0:T(8,128)(2,1)}, u32[]{:S(2)}, u32[]{:S(2)}) collective-permute-start(bf16[768,384]{1,0:T(8,128)(2,1)S(1)} %collective-permute-done.5), channel_id=1, source_target_pairs={{0,4},{4,8},{8,12},{12,16},{16,20},{20,24},{24,28},{28,0},{1,5},{5... | collective-permute-start | bytes 1769480 | tf_op jit(solution)/shard_map/ppermute | solution.py:64
  108.8 20.6 %copy-start = (bf16[3072,384]{1,0:T(8,128)(2,1)S(1)}, bf16[3072,384]{1,0:T(8,128)(2,1)}, u32[]{:S(2)}) copy-start(bf16[3072,384]{1,0:T(8,128)(2,1)} %param.11) | copy-start | bytes 7077892
  154.5 7.2 %copy-start.1 = (f32[768]{0:T(1024)S(1)}, f32[768]{0:T(1024)}, u32[]{:S(2)}) copy-start(f32[768]{0:T(1024)} %get-tuple-element.33) | copy-start | bytes 9220
  154.5 7.2 %copy-start.2 = (f32[768]{0:T(1024)S(1)}, f32[768]{0:T(1024)}, u32[]{:S(2)}) copy-start(f32[768]{0:T(1024)} %get-tuple-element.34) | copy-start | bytes 9220
  154.5 7.2 %copy-start.3 = (f32[768]{0:T(1024)S(1)}, f32[768]{0:T(1024)}, u32[]{:S(2)}) copy-start(f32[768]{0:T(1024)} %get-tuple-element.35) | copy-start | bytes 9220
  154.5 7.2 %copy-start.4 = (f32[768]{0:T(1024)S(1)}, f32[768]{0:T(1024)}, u32[]{:S(2)}) copy-start(f32[768]{0:T(1024)} %get-tuple-element.36) | copy-start | bytes 9220
  154.5 7.2 %copy-start.5 = (f32[768]{0:T(1024)S(1)}, f32[768]{0:T(1024)}, u32[]{:S(2)}) copy-start(f32[768]{0:T(1024)} %get-tuple-element.37) | copy-start | bytes 9220
  161.7 34.7 %copy-start.6 = (f32[1,4,8,41]{3,2,1,0:T(8,128)S(1)}, f32[1,4,8,41]{3,2,1,0:T(8,128)}, u32[]{:S(2)}) copy-start(f32[1,4,8,41]{3,2,1,0:T(8,128)} %param.15) | copy-start | bytes 15748
  161.7 35.0 %copy-start.7 = (s32[1,8,41]{2,1,0:T(8,128)S(1)}, s32[1,8,41]{2,1,0:T(8,128)}, u32[]{:S(2)}) copy-start(s32[1,8,41]{2,1,0:T(8,128)} %param.14) | copy-start | bytes 3940
  193.0 9.8 %all-to-all-start = ((s32[8,1,41]{2,1,0:T(1,128)}), s32[8,1,41]{2,1,0:T(1,128)S(1)}, u32[]{:S(2)}, u32[]{:S(2)}) async-start(s32[8,1,41]{2,1,0:T(1,128)} %bitcast.2), calls=%async_computation | async-start | bytes 8192 | tf_op jit(solution)/shard_map/all_to_all | solution.py:90
  204.3 12.6 %collective-permute-start.7 = (bf16[768,1,128]{0,2,1:T(8,128)(2,1)S(1)}, bf16[768,1,128]{0,2,1:T(8,128)(2,1)S(1)}, u32[]{:S(2)}, u32[]{:S(2)}) collective-permute-start(bf16[768,1,128]{0,2,1:T(8,128)(2,1)S(1)} %get-tuple-element.40), channel_id=1, source_target_pairs={{0,4},{4,8},{8,12},{12,16},{16,20},{20,24},{24,28},{28,0},{1,5},{5... | collective-permute-start | bytes 589832 | tf_op jit(solution)/shard_map/ppermute | solution.py:14
  204.8 12.1 %collective-permute-start.8 = (bf16[768,1,128]{0,2,1:T(8,128)(2,1)S(1)}, bf16[768,1,128]{0,2,1:T(8,128)(2,1)S(1)}, u32[]{:S(2)}, u32[]{:S(2)}) collective-permute-start(bf16[768,1,128]{0,2,1:T(8,128)(2,1)S(1)} %get-tuple-element.41), channel_id=1, source_target_pairs={{4,0},{8,4},{12,8},{16,12},{20,16},{24,20},{28,24},{0,28},{5,1},{9... | collective-permute-start | bytes 589832 | tf_op jit(solution)/shard_map/ppermute | solution.py:16
Sparse Core Ops, SparseCore 0:
  11.5 84.7 all-gather.3
  193.1 66.1 all-gather.5
